TPU v7x, 32 devices: a whole 2x2x4 slice. The times are simulated.
32 devices in a mesh: group: 4 (over y, core), dev: 8 (over z, x).
Axes of the slice: x: 2, y: 2, z: 4, core: 2. Of those that a mesh axis runs over, the one named last changes fastest.
Arguments:
- node_state: bfloat16 [16384, 512], P(('group', 'dev')), may hold values from -6 to 6
- hub_state: bfloat16 [64, 512], P('dev'), may hold values from -6 to 6
- w_edge_in: bfloat16 [512, 256], replicated, may hold values from -0.25 to 0.25
- w_edge_out: bfloat16 [256, 512], replicated, may hold values from -0.375 to 0.375
- w_update: bfloat16 [512, 512], replicated, may hold values from -0.25 to 0.25
- edge_src: int32 [131072], P(('group', 'dev')), may hold values from 0 to 319
- edge_dst: int32 [131072], P(('group', 'dev')), may hold values from 0 to 319
- edge_mask: int32 [131072], P(('group', 'dev')), may hold values 0 or 1
- send_list: int32 [32, 8, 32], P(('group', 'dev')), may hold values from 0 to 511
- send_count: int32 [32, 8], P(('group', 'dev')), may hold values from 8 to 32, as said below
- node_cot: bfloat16 [16384, 512], P(('group', 'dev')), may hold values from -0.059814453 to 0.059814453
- hub_cot: bfloat16 [64, 512], P('dev'), may hold values from -0.059814453 to 0.059814453
Outputs:
- new_state: bfloat16 [16384, 512], P(('group', 'dev'))
- new_hub: bfloat16 [64, 512], P('dev')
- grad_in: float32 [512, 256], replicated
- grad_out: float32 [256, 512], replicated
- grad_update: float32 [512, 512], replicated
Inputs may be any that keep to these rules, and one draw needn't show every extreme that they name: Device 0 sends 32 live slots to peer 0: send_count[0, 0] = 32.
All inputs are finite; a program needn't handle non-finite values. No bound on the sum of `edge_mask` on one device may be relied on, other than what follows from the above.
Results may differ from a plain program's by a relative error of at most 0.0064.
The roundings to bfloat16 on the way count: a program that leaves them out, or rounds other values in their place, can miss the bound.
Values may be sent and summed in bfloat16 or wider, within the bound.
No kernel may reach another device: no remote copies, remote signals or barrier semaphores. Data moves between devices by JAX's collectives and lax.ppermute only.
A program may use at most 64 MiB of HBM per device.

v0:
```python
import jax
import jax.numpy as jnp
from jax import lax
from jax.sharding import PartitionSpec as P


def silu_grad(values):
    sigmoid_v = jax.nn.sigmoid(values)
    return sigmoid_v * (1.0 + values * (1.0 - sigmoid_v))


def finish(states, summed, degree, w_update):
    mean_part = summed / jnp.maximum(degree, 1.0)[:, None]
    mixed_rows = (states.astype(jnp.float32) + mean_part).astype(jnp.bfloat16)
    pre_update = jnp.dot(mixed_rows, w_update, preferred_element_type=jnp.float32)
    updated = (states.astype(jnp.float32) + jax.nn.silu(pre_update)).astype(jnp.bfloat16)
    return (mixed_rows, pre_update, updated)


def backward_rows(cotangent, pre_update, degree, w_update):
    grad_pre = (cotangent.astype(jnp.float32) * silu_grad(pre_update)).astype(jnp.bfloat16)
    grad_mix = jnp.dot(grad_pre, w_update.T, preferred_element_type=jnp.float32)
    grad_sum = (grad_mix / jnp.maximum(degree, 1.0)[:, None]).astype(jnp.bfloat16)
    return (grad_pre, grad_sum)


def shards(
    node_state,
    hub_state,
    w_edge_in,
    w_edge_out,
    w_update,
    edge_src,
    edge_dst,
    edge_mask,
    send_list,
    send_count,
    node_cot,
    hub_cot,
):
    width = node_state.shape[1]
    master_rows = node_state.shape[0]
    send_rows = send_list[0]
    peer_total = send_rows.shape[0]
    slot_width = send_rows.shape[1]
    mirror_total = peer_total * slot_width
    live_slot = jnp.arange(slot_width)[None, :] < send_count[0][:, None]
    flat_rows = send_rows.reshape(-1)
    flat_live = live_slot.reshape(-1)
    selector = (
        (flat_rows[:, None] == jnp.arange(master_rows)[None, :]) & flat_live[:, None]
    ).astype(jnp.bfloat16)
    contract = (((0,), (0,)), ((), ()))
    outgoing = jnp.dot(selector, node_state, preferred_element_type=jnp.float32).astype(
        jnp.bfloat16
    )
    mirror_rows = lax.all_to_all(
        outgoing.reshape(peer_total, slot_width, width),
        "dev",
        split_axis=0,
        concat_axis=0,
        tiled=True,
    )
    hub_table = lax.all_gather(hub_state, "dev", axis=0, tiled=True)
    local_table = jnp.concatenate([mirror_rows.reshape(mirror_total, width), hub_table], axis=0)
    local_rows = local_table.shape[0]
    edge_total = edge_src.shape[0]
    block_size = min(1024, edge_total)
    block_count = edge_total // block_size
    sources = edge_src.reshape(block_count, block_size)
    targets = edge_dst.reshape(block_count, block_size)
    edge_keep = edge_mask.reshape(block_count, block_size)
    row_ids = jnp.arange(local_rows)[None, :]

    def forward_step(totals, pieces):
        source_ids, target_ids, keep_ids = pieces
        gathered = local_table[source_ids]
        pre_act = jnp.dot(gathered, w_edge_in, preferred_element_type=jnp.float32)
        hidden = jax.nn.silu(pre_act).astype(jnp.bfloat16)
        message = jnp.dot(hidden, w_edge_out, preferred_element_type=jnp.float32).astype(
            jnp.bfloat16
        )
        onehot = ((target_ids[:, None] == row_ids) & (keep_ids[:, None] > 0)).astype(jnp.bfloat16)
        added = lax.dot_general(onehot, message, contract, preferred_element_type=jnp.float32)
        tally = jnp.sum(onehot, axis=0, dtype=jnp.float32)
        return ((totals[0] + added, totals[1] + tally), pre_act)

    start_fwd = (jnp.zeros((local_rows, width), jnp.float32), jnp.zeros((local_rows,), jnp.float32))
    (partial_value, counts_local), saved_acts = lax.scan(
        forward_step, start_fwd, (sources, targets, edge_keep)
    )
    mirror_part = (
        partial_value[:mirror_total].reshape(peer_total, slot_width, width).astype(jnp.bfloat16)
    )
    mirror_count = counts_local[:mirror_total].reshape(peer_total, slot_width).astype(jnp.bfloat16)
    back_part, back_count = (
        lax.all_to_all(mirror_part, "dev", split_axis=0, concat_axis=0, tiled=True),
        lax.all_to_all(mirror_count, "dev", split_axis=0, concat_axis=0, tiled=True),
    )
    summed = lax.dot_general(
        selector,
        back_part.reshape(mirror_total, width),
        contract,
        preferred_element_type=jnp.float32,
    )
    degree = lax.dot_general(
        selector, back_count.reshape(mirror_total, 1), contract, preferred_element_type=jnp.float32
    )[:, 0]
    hub_part = partial_value[mirror_total:]
    hub_count = counts_local[mirror_total:]
    whole_part, whole_count = (
        lax.psum(hub_part.astype(jnp.bfloat16), "group").astype(jnp.float32),
        lax.psum(hub_count.astype(jnp.bfloat16), "group").astype(jnp.float32),
    )
    hub_summed, hub_degree = (
        lax.psum_scatter(
            whole_part.astype(jnp.bfloat16), "dev", scatter_dimension=0, tiled=True
        ).astype(jnp.float32),
        lax.psum_scatter(
            whole_count.astype(jnp.bfloat16), "dev", scatter_dimension=0, tiled=True
        ).astype(jnp.float32),
    )
    mixed_rows, pre_update, new_state = finish(node_state, summed, degree, w_update)
    hub_mixed, hub_pre, new_hub = finish(hub_state, hub_summed, hub_degree, w_update)
    grad_pre, grad_sum = backward_rows(node_cot, pre_update, degree, w_update)
    hub_grad_pre, hub_grad_sum = backward_rows(hub_cot, hub_pre, hub_degree, w_update)
    grad_outgoing = jnp.dot(selector, grad_sum, preferred_element_type=jnp.float32).astype(
        jnp.bfloat16
    )
    grad_mirror = lax.all_to_all(
        grad_outgoing.reshape(peer_total, slot_width, width),
        "dev",
        split_axis=0,
        concat_axis=0,
        tiled=True,
    )
    grad_hubs = lax.all_gather(hub_grad_sum, "dev", axis=0, tiled=True)
    grad_table = jnp.concatenate([grad_mirror.reshape(mirror_total, width), grad_hubs], axis=0)
    hub_weight = (lax.axis_index("group") == 0).astype(jnp.float32)
    grad_update = lax.dot_general(
        mixed_rows, grad_pre, contract, preferred_element_type=jnp.float32
    )
    grad_update = grad_update + hub_weight * lax.dot_general(
        hub_mixed, hub_grad_pre, contract, preferred_element_type=jnp.float32
    )

    def backward_step(totals, pieces):
        source_ids, target_ids, keep_ids, pre_act = pieces
        gathered = local_table[source_ids]
        hidden = jax.nn.silu(pre_act).astype(jnp.bfloat16)
        grad_message = jnp.where(
            keep_ids[:, None] > 0, grad_table[target_ids], jnp.zeros((), jnp.bfloat16)
        )
        grad_w_out = lax.dot_general(
            hidden, grad_message, contract, preferred_element_type=jnp.float32
        )
        grad_hidden = jnp.dot(grad_message, w_edge_out.T, preferred_element_type=jnp.float32)
        grad_act = (grad_hidden * silu_grad(pre_act)).astype(jnp.bfloat16)
        grad_w_in = lax.dot_general(
            gathered, grad_act, contract, preferred_element_type=jnp.float32
        )
        return ((totals[0] + grad_w_in, totals[1] + grad_w_out), None)

    start = (jnp.zeros(w_edge_in.shape, jnp.float32), jnp.zeros(w_edge_out.shape, jnp.float32))
    local_grads, _ = lax.scan(backward_step, start, (sources, targets, edge_keep, saved_acts))
    grad_in, grad_out, grad_upd = lax.psum(
        (local_grads[0], local_grads[1], grad_update), ("group", "dev")
    )
    return (new_state, new_hub, grad_in, grad_out, grad_upd)


def solution(mesh):
    return jax.shard_map(
        shards,
        mesh=mesh,
        in_specs=(
            P(("group", "dev"), None),
            P("dev", None),
            P(),
            P(),
            P(),
            P(("group", "dev")),
            P(("group", "dev")),
            P(("group", "dev")),
            P(("group", "dev"), None, None),
            P(("group", "dev"), None),
            P(("group", "dev"), None),
            P("dev", None),
        ),
        out_specs=(P(("group", "dev"), None), P("dev", None), P(), P(), P()),
        check_vma=False,
    )
```

profile of v0, /device:TPU:0, one launch (start us, length us, event | category | flops | bytes accessed | tf_op | source)
XLA Modules:
  0.0 417.0 jit_solution(8544541724577750692)
XLA Ops:
  7.2 0.8 iota_compare_fusion.2
  8.1 0.8 eq.35
  8.8 2.1 convolution_convert_fusion.1
  10.9 7.2 %all-to-all-start = ((bf16[8,32,512]{2,1,0:T(8,128)(2,1)}), bf16[8,32,512]{2,1,0:T(8,128)(2,1)S(1)}, u32[]{:S(2)}, u32[]{:S(2)}) async-start(bf16[8,32,512]{2,1,0:T(8,128)(2,1)} %bitcast.1), calls=%async_computation | async-start | bytes 524288 | tf_op jit(solution)/shard_map/all_to_all | solution.py:57
  18.2 0.7 reshape.192
  18.9 0.7 reshape.193
  19.7 0.7 reshape.194
  20.4 31.2 %all_gather.6 = bf16[64,512]{1,0:T(8,128)(2,1)S(1)} all-gather(bf16[8,512]{1,0:T(8,128)(2,1)} %param.17), channel_id=1, replica_groups=mesh['group'=4,'dev'=8] {'dev'}, dimensions={0}, use_global_device_ids=true | all-gather | bytes 73728 | tf_op jit(solution)/shard_map/all_gather | solution.py:64
  51.7 33.4 %while.28 = (s32[]{:T(128)}, f32[320,512]{1,0:T(8,128)}, f32[320]{0:T(512)S(1)}, f32[4,1024,256]{2,1,0:T(8,128)}, s32[4,1024]{1,0:T(4,128)S(1)}, /*index=5*/s32[...) while((s32[]{:T(128)}, f32[320,512]{1,0:T(8,128)}, ...), condition=%wide.region_2.3_spmd.clone, body=%wide.region_0.2_spmd.clone.sunk | while | flops 876877120 | bytes 10273476 | solution.py:89
  51.8 4.0 gather_fusion
  55.7 1.4 bitcast_dynamic-update-slice_fusion.2
  57.2 1.7 fusion.93
  58.9 0.3 convert_reduce_fusion.2
  59.3 4.0 gather_fusion
  63.3 1.5 bitcast_dynamic-update-slice_fusion.2
  64.8 2.7 fusion.93
  67.5 0.3 convert_reduce_fusion.2
  67.9 4.0 gather_fusion
  71.9 1.4 bitcast_dynamic-update-slice_fusion.2
  73.4 2.7 fusion.93
  76.1 0.3 convert_reduce_fusion.2
  76.5 4.0 gather_fusion
  80.5 1.4 bitcast_dynamic-update-slice_fusion.2
  82.0 2.7 fusion.93
  85.1 0.7 convert_element_type.118
  85.8 5.4 %all-to-all-start.2 = ((bf16[8,1,32]{2,1,0:T(2,128)(2,1)}), bf16[8,1,32]{2,1,0:T(2,128)(2,1)S(1)}, u32[]{:S(2)}, u32[]{:S(2)}) async-start(bf16[8,1,32]{2,1,0:T(2,128)(2,1)} %convert_element_type.118), calls=%async_computation.2 | async-start | bytes 8192 | tf_op jit(solution)/shard_map/all_to_all | solution.py:98
  91.3 0.6 dynamic-slice
  92.5 1.2 convert.8
  93.7 0.7 slice.34
  94.5 0.6 slice.35
  95.1 21.8 %all-reduce = bf16[64]{0:T(256)(128)(2,1)S(1)} all-reduce(bf16[64]{0:T(256)(128)(2,1)S(1)} %slice.27), channel_id=3, replica_groups=mesh['group'=4,'dev'=8] {'dev'}, use_global_device_ids=true, to_apply=%region_6.7.clone | all-reduce | flops 64 | bytes 256
  117.0 3.4 all-to-all-start.1
  120.8 38.2 %reduce-scatter.2.cloned.1.call-done = bf16[8,512]{1,0:T(8,128)(2,1)} async-done(((bf16[64,512]{1,0:T(8,128)(2,1)}), bf16[8,512]{1,0:T(8,128)(2,1)}) %reduce-scatter.2.cloned.1.call-update) | async-done | bytes 8208 | tf_op jit(solution)/shard_map/reduce_scatter | solution.py:116
  159.0 6.0 %all-reduce.2 = (bf16[8,512]{1,0:T(8,128)(2,1)S(1)}, bf16[8]{0:T(256)(128)(2,1)S(1)}) all-reduce(bf16[8,512]{1,0:T(8,128)(2,1)} %reduce-scatter.2.cloned.1.call-done, bf16[8]{0:T(256)(128)(2,1)S(1)} %dynamic-slice.1), channel_id=1, replica_groups=mesh['group'=4,'dev'=8] {'group'}, use_global_device_ids=true, to_apply=%region_3.4 | all-reduce | flops 4104 | bytes 16416 | tf_op jit(solution)/shard_map/psum | solution.py:112
  165.0 0.8 fusion.60
  166.1 30.5 %all_gather.7 = bf16[64,512]{1,0:T(8,128)(2,1)S(1)} all-gather(bf16[8,512]{1,0:T(8,128)(2,1)S(1)} %fusion.42), channel_id=1, replica_groups=mesh['group'=4,'dev'=8] {'dev'}, dimensions={0}, use_global_device_ids=true | all-gather | bytes 73728 | tf_op jit(solution)/shard_map/all_gather | solution.py:137
  196.6 1.5 fusion.38
  198.2 2.7 multiply_convert_fusion.3
  200.9 1.4 fusion.41
  202.3 3.6 all-to-all-start.3
  205.9 0.5 fusion.64
  206.4 1.4 fusion.36
  207.8 6.3 %all-to-all-done.3 = bf16[8,32,512]{2,1,0:T(8,128)(2,1)S(1)} async-done(((bf16[8,32,512]{2,1,0:T(8,128)(2,1)}), bf16[8,32,512]{2,1,0:T(8,128)(2,1)S(1)}, u32[]{:S(2)}, u32[]{:S(2)}) %all-to-all-start.3) | async-done | bytes 262176 | tf_op jit(solution)/shard_map/all_to_all | solution.py:130
  214.1 56.7 %while.29 = (s32[]{:T(128)}, f32[512,256]{1,0:T(8,128)}, f32[256,512]{1,0:T(8,128)}, s32[4,1024]{1,0:T(4,128)S(1)}, bf16[320,512]{1,0:T(8,128)(2,1)S(1)}, /*inde...) while((s32[]{:T(128)}, f32[512,256]{1,0:T(8,128)}, ...), condition=%wide.region_8.9_spmd.clone, body=%wide.region_7.8_spmd.clone.sunk | while | flops 810558464 | bytes 11845768 | solution.py:165
  214.2 4.0 gather_fusion.2
  218.2 4.0 gather_fusion.1
  222.2 3.3 convolution_add_fusion.4
  225.5 2.6 convolution_add_fusion.5
  228.1 4.0 gather_fusion.2
  232.1 4.0 gather_fusion.1
  236.1 3.4 convolution_add_fusion.4
  239.6 2.8 convolution_add_fusion.5
  242.4 4.0 gather_fusion.2
  246.3 4.0 gather_fusion.1
  250.4 3.4 convolution_add_fusion.4
  253.8 2.8 convolution_add_fusion.5
  256.6 4.0 gather_fusion.2
  260.6 4.0 gather_fusion.1
  264.6 3.4 convolution_add_fusion.4
  268.0 2.7 convolution_add_fusion.5
  270.8 133.3 %all-reduce.5.cloned.1.call-done = (f32[512,256]{1,0:T(8,128)}, f32[256,512]{1,0:T(8,128)}, f32[512,512]{1,0:T(8,128)}) async-done(((f32[512,256]{1,0:T(8,128)}, f32[256,512]{1,0:T(8,128)}, f32[512,512]{1,0:T(8,128)}), (f32[512,256]{1,0:T(8,128)}, f32[256,512]{1,0:T(8,128)}, f32[512,512]{1,0:T(8,128)})) %all-reduce.5.cloned.1.call-update) | async-done | bytes 2097168 | tf_op jit(solution)/shard_map/psum | solution.py:166
  404.1 1.9 copy.44
  406.0 1.9 copy.45
  407.9 2.3 copy.46
  (88 shorter events, 1.9 us)
Async XLA Ops:
  7.2 157.8 %copy-start = (bf16[512,512]{1,0:T(8,128)(2,1)S(1)}, bf16[512,512]{1,0:T(8,128)(2,1)}, u32[]{:S(2)}) copy-start(bf16[512,512]{1,0:T(8,128)(2,1)} %param.20) | copy-start | bytes 1572868
  10.9 40.7 %all-to-all-start = ((bf16[8,32,512]{2,1,0:T(8,128)(2,1)}), bf16[8,32,512]{2,1,0:T(8,128)(2,1)S(1)}, u32[]{:S(2)}, u32[]{:S(2)}) async-start(bf16[8,32,512]{2,1,0:T(8,128)(2,1)} %bitcast.1), calls=%async_computation | async-start | bytes 524288 | tf_op jit(solution)/shard_map/all_to_all | solution.py:57
  51.7 39.6 %copy-start.6 = (u32[32]{0:T(128)S(1)}, u32[32]{0:T(128)}, u32[]{:S(2)}) copy-start(u32[32]{0:T(128)} %constant.65) | copy-start | bytes 388
  51.7 113.3 %copy-start.2 = (bf16[8,512]{1,0:T(8,128)(2,1)S(1)}, bf16[8,512]{1,0:T(8,128)(2,1)}, u32[]{:S(2)}) copy-start(bf16[8,512]{1,0:T(8,128)(2,1)} %param.17) | copy-start | bytes 24580
  51.7 114.2 %copy-start.3 = (bf16[8,512]{1,0:T(8,128)(2,1)S(1)}, bf16[8,512]{1,0:T(8,128)(2,1)}, u32[]{:S(2)}) copy-start(bf16[8,512]{1,0:T(8,128)(2,1)} %param.27) | copy-start | bytes 24580
  51.7 4.0 copy-start.1
  51.8 5.5 %copy-start.5 = (bf16[256,512]{1,0:T(8,128)(2,1)S(1)}, bf16[256,512]{1,0:T(8,128)(2,1)}, u32[]{:S(2)}) copy-start(bf16[256,512]{1,0:T(8,128)(2,1)} %get-tuple-element.406) | copy-start | bytes 786436 | tf_op jit(solution)/shard_map/while
  59.2 4.0 copy-start.1
  59.3 5.5 %copy-start.5 = (bf16[256,512]{1,0:T(8,128)(2,1)S(1)}, bf16[256,512]{1,0:T(8,128)(2,1)}, u32[]{:S(2)}) copy-start(bf16[256,512]{1,0:T(8,128)(2,1)} %get-tuple-element.406) | copy-start | bytes 786436 | tf_op jit(solution)/shard_map/while
  67.9 4.0 copy-start.1
  67.9 5.5 %copy-start.5 = (bf16[256,512]{1,0:T(8,128)(2,1)S(1)}, bf16[256,512]{1,0:T(8,128)(2,1)}, u32[]{:S(2)}) copy-start(bf16[256,512]{1,0:T(8,128)(2,1)} %get-tuple-element.406) | copy-start | bytes 786436 | tf_op jit(solution)/shard_map/while
  76.5 4.0 copy-start.1
  76.5 5.5 %copy-start.5 = (bf16[256,512]{1,0:T(8,128)(2,1)S(1)}, bf16[256,512]{1,0:T(8,128)(2,1)}, u32[]{:S(2)}) copy-start(bf16[256,512]{1,0:T(8,128)(2,1)} %get-tuple-element.406) | copy-start | bytes 786436 | tf_op jit(solution)/shard_map/while
  85.8 31.2 %all-to-all-start.2 = ((bf16[8,1,32]{2,1,0:T(2,128)(2,1)}), bf16[8,1,32]{2,1,0:T(2,128)(2,1)S(1)}, u32[]{:S(2)}, u32[]{:S(2)}) async-start(bf16[8,1,32]{2,1,0:T(2,128)(2,1)} %convert_element_type.118), calls=%async_computation.2 | async-start | bytes 8192 | tf_op jit(solution)/shard_map/all_to_all | solution.py:98
  91.2 67.8 %reduce-scatter.2.cloned.1.call-start = ((), (), s32[]{:S(2)}) async-start(), calls=%async_computation.5 | async-start | bytes 73728 | tf_op jit(solution)/shard_map/reduce_scatter | solution.py:116
  92.5 105.6 %copy-start.4 = (bf16[512,512]{1,0:T(8,128)(2,1)S(1)}, bf16[512,512]{1,0:T(8,128)(2,1)}, u32[]{:S(2)}) copy-start(bf16[512,512]{1,0:T(8,128)(2,1)} %param.26) | copy-start | bytes 1572868
  117.0 79.6 %all-to-all-start.1 = ((bf16[8,32,512]{2,1,0:T(8,128)(2,1)}), bf16[8,32,512]{2,1,0:T(8,128)(2,1)S(1)}, u32[]{:S(2)}, u32[]{:S(2)}) async-start(bf16[8,32,512]{2,1,0:T(8,128)(2,1)} %bitcast.3), calls=%async_computation.1 | async-start | bytes 524288 | tf_op jit(solution)/shard_map/all_to_all | solution.py:97
  202.3 11.8 %all-to-all-start.3 = ((bf16[8,32,512]{2,1,0:T(8,128)(2,1)}), bf16[8,32,512]{2,1,0:T(8,128)(2,1)S(1)}, u32[]{:S(2)}, u32[]{:S(2)}) async-start(bf16[8,32,512]{2,1,0:T(8,128)(2,1)} %bitcast.6), calls=%async_computation.3 | async-start | bytes 524288 | tf_op jit(solution)/shard_map/all_to_all | solution.py:130
  205.9 198.3 %all-reduce.5.cloned.1.call-start = ((), (), s32[]{:S(2)}) async-start(), calls=%async_computation.6 | async-start | bytes 4194304 | tf_op jit(solution)/shard_map/psum | solution.py:166
Sparse Core Ops, SparseCore 0:
  96.0 62.9 reduce-scatter.1
  270.9 133.1 all-reduce.4
where the time goes:
time: 418 us; the launch traced here: 417 us
  waiting for transfers between devices  178 us (43%)
  blocking collectives  89.5 us (21%)
  local copies, waits for them, and re-layouts  59.5 us (14%)
  matrix products  51.1 us (12%)
  starting transfers between devices  19.8 us (5%)
  between operations  14.9 us (4%)
    psum x1, waiting for transfers between devices, shards(): lax.psum((local_grads[0], local_grads[1], grad_update), ('group', 'dev'))  133 us
    reduce_scatter x1, waiting for transfers between devices, shards(): lax.psum_scatter(whole_part.astype(jnp.bfloat16), 'dev', scatter_dimensio...  38.2 us
    all_gather x1, blocking collectives, shards(): hub_table = lax.all_gather(hub_state, 'dev', axis=0, tiled=True)  31.2 us
    all_gather x1, blocking collectives, shards(): grad_hubs = lax.all_gather(hub_grad_sum, 'dev', axis=0, tiled=True)  30.5 us
    unnamed x1, blocking collectives  21.8 us
    gather x4, local copies, waits for them, and re-layouts, backward_step(): grad_table[target_ids]  15.9 us
    gather x4, local copies, waits for them, and re-layouts, backward_step(): gathered = local_table[source_ids]  15.9 us
    gather x4, local copies, waits for them, and re-layouts, forward_step(): gathered = local_table[source_ids]  15.9 us
  transfers between devices with their start and end apart: 6, of which 3 were waited for; matrix products, arithmetic and copies ran while one was open for 2% of the time, Pallas kernels for 0%

commit v1 on v0

--- a/solution.py
+++ b/solution.py
@@ -134,7 +134,25 @@
         concat_axis=0,
         tiled=True,
     )
-    grad_hubs = lax.all_gather(hub_grad_sum, "dev", axis=0, tiled=True)
+    count, index, rows = (lax.axis_size("dev"), lax.axis_index("dev"), hub_grad_sum.shape[0])
+    upward = [(i, (i + 1) % count) for i in range(count)]
+    backward = [(i, (i - 1) % count) for i in range(count)]
+    grad_hubs = jnp.zeros(
+        (*hub_grad_sum.shape[:0], count * rows, *hub_grad_sum.shape[0 + 1 :]), hub_grad_sum.dtype
+    )
+    grad_hubs = lax.dynamic_update_slice_in_dim(grad_hubs, hub_grad_sum, index * rows, axis=0)
+    from_left = from_right = hub_grad_sum
+    halfway = count // 2
+    for step in range(1, halfway + 1):
+        from_left = lax.ppermute(from_left, "dev", upward)
+        grad_hubs = lax.dynamic_update_slice_in_dim(
+            grad_hubs, from_left, (index - step) % count * rows, axis=0
+        )
+        if step < count - halfway:
+            from_right = lax.ppermute(from_right, "dev", backward)
+            grad_hubs = lax.dynamic_update_slice_in_dim(
+                grad_hubs, from_right, (index + step) % count * rows, axis=0
+            )
     grad_table = jnp.concatenate([grad_mirror.reshape(mirror_total, width), grad_hubs], axis=0)
     hub_weight = (lax.axis_index("group") == 0).astype(jnp.float32)
     grad_update = lax.dot_general(

time: 418 us -> 414 us (level)
  blocking collectives: 89.5 us -> 58.9 us
  starting transfers between devices: 19.8 us -> 33.8 us
  waiting for transfers between devices: 178 us -> 189 us
    all_gather x1 -> x0, blocking collectives: 30.5 us -> none  [shards(): grad_hubs = lax.all_gather(hub_grad_sum, 'dev', axis=0, tiled=True)]
    ppermute x0 -> x7, starting transfers between devices: none -> 14.2 us  [the longest x3 12.7 us: shards(): from_right = lax.ppermute(from_right, 'dev', backward)]
    ppermute x0 -> x7, waiting for transfers between devices: none -> 11.2 us  [the longest x4 11.2 us: shards(): from_left = lax.ppermute(from_left, 'dev', upward)]
  transfers between devices with their start and end apart: 6 -> 13, of which waited for: 3 -> 7; matrix products, arithmetic and copies ran while one was open for 2% -> 2% of each run, Pallas kernels for 0% -> 0%
where the time goes in v1:
time: 414 us; the launch traced here: 413 us
  waiting for transfers between devices  189 us (46%)
  local copies, waits for them, and re-layouts  60.3 us (15%)
  blocking collectives  58.9 us (14%)
  matrix products  51.2 us (12%)
  starting transfers between devices  33.8 us (8%)
  between operations  15.1 us (4%)
    psum x1, waiting for transfers between devices, shards(): lax.psum((local_grads[0], local_grads[1], grad_update), ('group', 'dev'))  133 us
    reduce_scatter x1, waiting for transfers between devices, shards(): lax.psum_scatter(whole_part.astype(jnp.bfloat16), 'dev', scatter_dimensio...  38.7 us
    all_gather x1, blocking collectives, shards(): hub_table = lax.all_gather(hub_state, 'dev', axis=0, tiled=True)  31.1 us
    unnamed x1, blocking collectives  21.8 us
    gather x4, local copies, waits for them, and re-layouts, backward_step(): grad_table[target_ids]  15.9 us
    gather x4, local copies, waits for them, and re-layouts, forward_step(): gathered = local_table[source_ids]  15.9 us
    gather x4, local copies, waits for them, and re-layouts, backward_step(): gathered = local_table[source_ids]  15.9 us
    dot_general x4, matrix products, backward_step(): lax.dot_general(gathered, grad_act, contract, preferred_element_type=jnp....  13.8 us
  transfers between devices with their start and end apart: 13, of which 7 were waited for; matrix products, arithmetic and copies ran while one was open for 2% of the time, Pallas kernels for 0%

profile of v1, /device:TPU:0, one launch (start us, length us, event | category | flops | bytes accessed | tf_op | source)
XLA Modules:
  0.0 413.0 jit_solution(1058595964766229551)
XLA Ops:
  7.2 0.8 iota_compare_fusion.2
  8.1 0.8 eq.43
  8.8 2.1 convolution_convert_fusion.1
  10.9 7.2 %all-to-all-start = ((bf16[8,32,512]{2,1,0:T(8,128)(2,1)}), bf16[8,32,512]{2,1,0:T(8,128)(2,1)S(1)}, u32[]{:S(2)}, u32[]{:S(2)}) async-start(bf16[8,32,512]{2,1,0:T(8,128)(2,1)} %bitcast.1), calls=%async_computation | async-start | bytes 524288 | tf_op jit(solution)/shard_map/all_to_all | solution.py:57
  18.3 0.7 reshape.192
  19.1 0.7 reshape.193
  19.8 0.7 reshape.194
  20.5 1.3 dynamic-slice
  21.8 31.1 %all_gather.3 = bf16[64,512]{1,0:T(8,128)(2,1)S(1)} all-gather(bf16[8,512]{1,0:T(8,128)(2,1)} %param.17), channel_id=1, replica_groups=mesh['group'=4,'dev'=8] {'dev'}, dimensions={0}, use_global_device_ids=true | all-gather | bytes 73728 | tf_op jit(solution)/shard_map/all_gather | solution.py:64
  53.0 33.3 %while.28 = (s32[]{:T(128)}, f32[320,512]{1,0:T(8,128)}, f32[320]{0:T(512)S(1)}, f32[4,1024,256]{2,1,0:T(8,128)}, s32[4,1024]{1,0:T(4,128)S(1)}, /*index=5*/s32[...) while((s32[]{:T(128)}, f32[320,512]{1,0:T(8,128)}, ...), condition=%wide.region_2.3_spmd.clone, body=%wide.region_0.2_spmd.clone.sunk | while | flops 876877120 | bytes 10273476 | solution.py:89
  53.1 4.0 gather_fusion
  57.0 1.4 bitcast_dynamic-update-slice_fusion.2
  58.5 1.7 fusion.93
  60.6 4.0 gather_fusion
  64.6 1.4 bitcast_dynamic-update-slice_fusion.2
  66.1 2.7 fusion.93
  69.2 4.0 gather_fusion
  73.2 1.4 bitcast_dynamic-update-slice_fusion.2
  74.6 2.7 fusion.93
  77.8 4.0 gather_fusion
  81.8 1.4 bitcast_dynamic-update-slice_fusion.2
  83.2 2.7 fusion.93
  87.0 5.4 %all-to-all-start.2 = ((bf16[8,1,32]{2,1,0:T(2,128)(2,1)}), bf16[8,1,32]{2,1,0:T(2,128)(2,1)S(1)}, u32[]{:S(2)}, u32[]{:S(2)}) async-start(bf16[8,1,32]{2,1,0:T(2,128)(2,1)} %convert_element_type.118), calls=%async_computation.2 | async-start | bytes 8192 | tf_op jit(solution)/shard_map/all_to_all | solution.py:98
  93.2 1.2 convert.8
  95.8 21.8 %all-reduce = bf16[64]{0:T(256)(128)(2,1)S(1)} all-reduce(bf16[64]{0:T(256)(128)(2,1)S(1)} %slice.27), channel_id=3, replica_groups=mesh['group'=4,'dev'=8] {'dev'}, use_global_device_ids=true, to_apply=%region_6.7.clone | all-reduce | flops 64 | bytes 256
  117.7 3.4 all-to-all-start.1
  121.5 38.7 %reduce-scatter.2.cloned.1.call-done = bf16[8,512]{1,0:T(8,128)(2,1)} async-done(((bf16[64,512]{1,0:T(8,128)(2,1)}), bf16[8,512]{1,0:T(8,128)(2,1)}) %reduce-scatter.2.cloned.1.call-update) | async-done | bytes 8208 | tf_op jit(solution)/shard_map/reduce_scatter | solution.py:116
  160.3 6.0 %all-reduce.2 = (bf16[8,512]{1,0:T(8,128)(2,1)S(1)}, bf16[8]{0:T(256)(128)(2,1)S(1)}) all-reduce(bf16[8,512]{1,0:T(8,128)(2,1)} %reduce-scatter.2.cloned.1.call-done, bf16[8]{0:T(256)(128)(2,1)S(1)} %dynamic-slice.1), channel_id=1, replica_groups=mesh['group'=4,'dev'=8] {'group'}, use_global_device_ids=true, to_apply=%region_3.4 | all-reduce | flops 4104 | bytes 16416 | tf_op jit(solution)/shard_map/psum | solution.py:112
  166.3 0.8 fusion.60
  167.4 1.4 collective-permute-start
  168.8 3.3 collective-permute-start.1
  172.1 1.6 collective-permute-done
  173.8 4.7 %collective-permute-start.3 = (bf16[8,512]{1,0:T(8,128)(2,1)S(1)}, bf16[8,512]{1,0:T(8,128)(2,1)S(1)}, u32[]{:S(2)}, u32[]{:S(2)}) collective-permute-start(bf16[8,512]{1,0:T(8,128)(2,1)S(1)} %collective-permute-done.1), channel_id=1, source_target_pairs={{0,7},{1,0},{2,1},{3,2},{4,3},{5,4},{6,5},{7,6},{8,15},{9,8},{10,9... | collective-permute-start | bytes 24584 | tf_op jit(solution)/shard_map/ppermute | solution.py:152
  178.5 1.6 collective-permute-done.2
  180.1 4.7 %collective-permute-start.5 = (bf16[8,512]{1,0:T(8,128)(2,1)S(1)}, bf16[8,512]{1,0:T(8,128)(2,1)S(1)}, u32[]{:S(2)}, u32[]{:S(2)}) collective-permute-start(bf16[8,512]{1,0:T(8,128)(2,1)S(1)} %collective-permute-done.3), channel_id=1, source_target_pairs={{0,7},{1,0},{2,1},{3,2},{4,3},{5,4},{6,5},{7,6},{8,15},{9,8},{10,9... | collective-permute-start | bytes 24584 | tf_op jit(solution)/shard_map/ppermute | solution.py:152
  184.8 1.6 collective-permute-done.4
  186.5 6.3 %collective-permute-done.6 = bf16[8,512]{1,0:T(8,128)(2,1)S(1)} collective-permute-done((bf16[8,512]{1,0:T(8,128)(2,1)S(1)}, bf16[8,512]{1,0:T(8,128)(2,1)S(1)}, u32[]{:S(2)}, u32[]{:S(2)}) %collective-permute-start.6) | collective-permute-done | bytes 8224 | tf_op jit(solution)/shard_map/ppermute | solution.py:147
  192.8 1.5 fusion.38
  194.4 2.7 multiply_convert_fusion.3
  197.1 1.4 fusion.41
  198.5 3.4 all-to-all-start.3
  202.4 1.4 fusion.36
  203.8 6.3 %all-to-all-done.3 = bf16[8,32,512]{2,1,0:T(8,128)(2,1)S(1)} async-done(((bf16[8,32,512]{2,1,0:T(8,128)(2,1)}), bf16[8,32,512]{2,1,0:T(8,128)(2,1)S(1)}, u32[]{:S(2)}, u32[]{:S(2)}) %all-to-all-start.3) | async-done | bytes 262176 | tf_op jit(solution)/shard_map/all_to_all | solution.py:130
  210.1 56.9 %while.29 = (s32[]{:T(128)}, f32[512,256]{1,0:T(8,128)}, f32[256,512]{1,0:T(8,128)}, s32[4,1024]{1,0:T(4,128)S(1)}, bf16[320,512]{1,0:T(8,128)(2,1)S(1)}, /*inde...) while((s32[]{:T(128)}, f32[512,256]{1,0:T(8,128)}, ...), condition=%wide.region_8.9_spmd.clone, body=%wide.region_7.8_spmd.clone.sunk | while | flops 810558464 | bytes 11845768 | solution.py:183
  210.1 4.0 gather_fusion.2
  214.1 4.0 gather_fusion.1
  218.1 3.4 convolution_add_fusion.4
  221.5 2.6 convolution_add_fusion.5
  224.1 4.0 gather_fusion.2
  228.1 4.0 gather_fusion.1
  232.1 3.5 convolution_add_fusion.4
  235.6 2.8 convolution_add_fusion.5
  238.4 4.0 gather_fusion.2
  242.4 4.0 gather_fusion.1
  246.4 3.5 convolution_add_fusion.4
  249.9 2.8 convolution_add_fusion.5
  252.7 4.0 gather_fusion.2
  256.7 4.0 gather_fusion.1
  260.7 3.5 convolution_add_fusion.4
  264.2 2.8 convolution_add_fusion.5
  267.0 133.2 %all-reduce.5.cloned.1.call-done = (f32[512,256]{1,0:T(8,128)}, f32[256,512]{1,0:T(8,128)}, f32[512,512]{1,0:T(8,128)}) async-done(((f32[512,256]{1,0:T(8,128)}, f32[256,512]{1,0:T(8,128)}, f32[512,512]{1,0:T(8,128)}), (f32[512,256]{1,0:T(8,128)}, f32[256,512]{1,0:T(8,128)}, f32[512,512]{1,0:T(8,128)})) %all-reduce.5.cloned.1.call-update) | async-done | bytes 2097168 | tf_op jit(solution)/shard_map/psum | solution.py:184
  400.2 1.9 copy.52
  402.0 1.9 copy.53
  403.9 2.3 copy.54
  (107 shorter events, 5.4 us)
Async XLA Ops:
  7.2 159.1 %copy-start = (bf16[512,512]{1,0:T(8,128)(2,1)S(1)}, bf16[512,512]{1,0:T(8,128)(2,1)}, u32[]{:S(2)}) copy-start(bf16[512,512]{1,0:T(8,128)(2,1)} %param.20) | copy-start | bytes 1572868
  10.9 42.0 %all-to-all-start = ((bf16[8,32,512]{2,1,0:T(8,128)(2,1)}), bf16[8,32,512]{2,1,0:T(8,128)(2,1)S(1)}, u32[]{:S(2)}, u32[]{:S(2)}) async-start(bf16[8,32,512]{2,1,0:T(8,128)(2,1)} %bitcast.1), calls=%async_computation | async-start | bytes 524288 | tf_op jit(solution)/shard_map/all_to_all | solution.py:57
  53.0 113.3 %copy-start.2 = (bf16[8,512]{1,0:T(8,128)(2,1)S(1)}, bf16[8,512]{1,0:T(8,128)(2,1)}, u32[]{:S(2)}) copy-start(bf16[8,512]{1,0:T(8,128)(2,1)} %param.17) | copy-start | bytes 24580
  53.0 114.2 %copy-start.3 = (bf16[8,512]{1,0:T(8,128)(2,1)S(1)}, bf16[8,512]{1,0:T(8,128)(2,1)}, u32[]{:S(2)}) copy-start(bf16[8,512]{1,0:T(8,128)(2,1)} %param.27) | copy-start | bytes 24580
  53.0 4.0 copy-start.1
  53.0 5.5 %copy-start.5 = (bf16[256,512]{1,0:T(8,128)(2,1)S(1)}, bf16[256,512]{1,0:T(8,128)(2,1)}, u32[]{:S(2)}) copy-start(bf16[256,512]{1,0:T(8,128)(2,1)} %get-tuple-element.408) | copy-start | bytes 786436 | tf_op jit(solution)/shard_map/while
  60.5 4.0 copy-start.1
  60.6 5.5 %copy-start.5 = (bf16[256,512]{1,0:T(8,128)(2,1)S(1)}, bf16[256,512]{1,0:T(8,128)(2,1)}, u32[]{:S(2)}) copy-start(bf16[256,512]{1,0:T(8,128)(2,1)} %get-tuple-element.408) | copy-start | bytes 786436 | tf_op jit(solution)/shard_map/while
  69.2 4.0 copy-start.1
  69.2 5.5 %copy-start.5 = (bf16[256,512]{1,0:T(8,128)(2,1)S(1)}, bf16[256,512]{1,0:T(8,128)(2,1)}, u32[]{:S(2)}) copy-start(bf16[256,512]{1,0:T(8,128)(2,1)} %get-tuple-element.408) | copy-start | bytes 786436 | tf_op jit(solution)/shard_map/while
  77.7 4.0 copy-start.1
  77.8 5.5 %copy-start.5 = (bf16[256,512]{1,0:T(8,128)(2,1)S(1)}, bf16[256,512]{1,0:T(8,128)(2,1)}, u32[]{:S(2)}) copy-start(bf16[256,512]{1,0:T(8,128)(2,1)} %get-tuple-element.408) | copy-start | bytes 786436 | tf_op jit(solution)/shard_map/while
  87.0 30.7 %all-to-all-start.2 = ((bf16[8,1,32]{2,1,0:T(2,128)(2,1)}), bf16[8,1,32]{2,1,0:T(2,128)(2,1)S(1)}, u32[]{:S(2)}, u32[]{:S(2)}) async-start(bf16[8,1,32]{2,1,0:T(2,128)(2,1)} %convert_element_type.118), calls=%async_computation.2 | async-start | bytes 8192 | tf_op jit(solution)/shard_map/all_to_all | solution.py:98
  92.4 67.8 %reduce-scatter.2.cloned.1.call-start = ((), (), s32[]{:S(2)}) async-start(), calls=%async_computation.5 | async-start | bytes 73728 | tf_op jit(solution)/shard_map/reduce_scatter | solution.py:116
  93.2 101.1 %copy-start.4 = (bf16[512,512]{1,0:T(8,128)(2,1)S(1)}, bf16[512,512]{1,0:T(8,128)(2,1)}, u32[]{:S(2)}) copy-start(bf16[512,512]{1,0:T(8,128)(2,1)} %param.26) | copy-start | bytes 1572868
  117.7 75.1 %all-to-all-start.1 = ((bf16[8,32,512]{2,1,0:T(8,128)(2,1)}), bf16[8,32,512]{2,1,0:T(8,128)(2,1)S(1)}, u32[]{:S(2)}, u32[]{:S(2)}) async-start(bf16[8,32,512]{2,1,0:T(8,128)(2,1)} %bitcast.3), calls=%async_computation.1 | async-start | bytes 524288 | tf_op jit(solution)/shard_map/all_to_all | solution.py:97
  167.4 6.4 %collective-permute-start = (bf16[8,512]{1,0:T(8,128)(2,1)S(1)}, bf16[8,512]{1,0:T(8,128)(2,1)S(1)}, u32[]{:S(2)}, u32[]{:S(2)}) collective-permute-start(bf16[8,512]{1,0:T(8,128)(2,1)S(1)} %get-tuple-element.244), channel_id=1, source_target_pairs={{0,1},{1,2},{2,3},{3,4},{4,5},{5,6},{6,7},{7,0},{8,9},{9,10},{10,1... | collective-permute-start | bytes 24584 | tf_op jit(solution)/shard_map/ppermute | solution.py:147
  168.8 4.9 %collective-permute-start.1 = (bf16[8,512]{1,0:T(8,128)(2,1)S(1)}, bf16[8,512]{1,0:T(8,128)(2,1)S(1)}, u32[]{:S(2)}, u32[]{:S(2)}) collective-permute-start(bf16[8,512]{1,0:T(8,128)(2,1)S(1)} %get-tuple-element.244), channel_id=1, source_target_pairs={{0,7},{1,0},{2,1},{3,2},{4,3},{5,4},{6,5},{7,6},{8,15},{9,8},{10,9... | collective-permute-start | bytes 24584 | tf_op jit(solution)/shard_map/ppermute | solution.py:152
  173.8 6.3 %collective-permute-start.2 = (bf16[8,512]{1,0:T(8,128)(2,1)S(1)}, bf16[8,512]{1,0:T(8,128)(2,1)S(1)}, u32[]{:S(2)}, u32[]{:S(2)}) collective-permute-start(bf16[8,512]{1,0:T(8,128)(2,1)S(1)} %collective-permute-done), channel_id=1, source_target_pairs={{0,1},{1,2},{2,3},{3,4},{4,5},{5,6},{6,7},{7,0},{8,9},{9,10},{10,1... | collective-permute-start | bytes 24584 | tf_op jit(solution)/shard_map/ppermute | solution.py:147
  173.8 6.3 %collective-permute-start.3 = (bf16[8,512]{1,0:T(8,128)(2,1)S(1)}, bf16[8,512]{1,0:T(8,128)(2,1)S(1)}, u32[]{:S(2)}, u32[]{:S(2)}) collective-permute-start(bf16[8,512]{1,0:T(8,128)(2,1)S(1)} %collective-permute-done.1), channel_id=1, source_target_pairs={{0,7},{1,0},{2,1},{3,2},{4,3},{5,4},{6,5},{7,6},{8,15},{9,8},{10,9... | collective-permute-start | bytes 24584 | tf_op jit(solution)/shard_map/ppermute | solution.py:152
  180.1 6.3 %collective-permute-start.4 = (bf16[8,512]{1,0:T(8,128)(2,1)S(1)}, bf16[8,512]{1,0:T(8,128)(2,1)S(1)}, u32[]{:S(2)}, u32[]{:S(2)}) collective-permute-start(bf16[8,512]{1,0:T(8,128)(2,1)S(1)} %collective-permute-done.2), channel_id=1, source_target_pairs={{0,1},{1,2},{2,3},{3,4},{4,5},{5,6},{6,7},{7,0},{8,9},{9,10},{10,1... | collective-permute-start | bytes 24584 | tf_op jit(solution)/shard_map/ppermute | solution.py:147
  180.1 6.3 %collective-permute-start.5 = (bf16[8,512]{1,0:T(8,128)(2,1)S(1)}, bf16[8,512]{1,0:T(8,128)(2,1)S(1)}, u32[]{:S(2)}, u32[]{:S(2)}) collective-permute-start(bf16[8,512]{1,0:T(8,128)(2,1)S(1)} %collective-permute-done.3), channel_id=1, source_target_pairs={{0,7},{1,0},{2,1},{3,2},{4,3},{5,4},{6,5},{7,6},{8,15},{9,8},{10,9... | collective-permute-start | bytes 24584 | tf_op jit(solution)/shard_map/ppermute | solution.py:152
  186.5 6.3 %collective-permute-start.6 = (bf16[8,512]{1,0:T(8,128)(2,1)S(1)}, bf16[8,512]{1,0:T(8,128)(2,1)S(1)}, u32[]{:S(2)}, u32[]{:S(2)}) collective-permute-start(bf16[8,512]{1,0:T(8,128)(2,1)S(1)} %collective-permute-done.4), channel_id=1, source_target_pairs={{0,1},{1,2},{2,3},{3,4},{4,5},{5,6},{6,7},{7,0},{8,9},{9,10},{10,1... | collective-permute-start | bytes 24584 | tf_op jit(solution)/shard_map/ppermute | solution.py:147
  198.5 11.6 %all-to-all-start.3 = ((bf16[8,32,512]{2,1,0:T(8,128)(2,1)}), bf16[8,32,512]{2,1,0:T(8,128)(2,1)S(1)}, u32[]{:S(2)}, u32[]{:S(2)}) async-start(bf16[8,32,512]{2,1,0:T(8,128)(2,1)} %bitcast.6), calls=%async_computation.3 | async-start | bytes 524288 | tf_op jit(solution)/shard_map/all_to_all | solution.py:130
  201.9 198.3 %all-reduce.5.cloned.1.call-start = ((), (), s32[]{:S(2)}) async-start(), calls=%async_computation.6 | async-start | bytes 4194304 | tf_op jit(solution)/shard_map/psum | solution.py:184
Sparse Core Ops, SparseCore 0:
  97.2 62.9 reduce-scatter.1
  267.1 133.0 all-reduce.4
